TPU v7x, 256 devices: a whole 4x4x8 slice. The times are simulated.
256 devices in a mesh: gx: 32 (over y, z), gy: 8 (over x, core).
Axes of the slice: x: 4, y: 4, z: 8, core: 2. Of those that a mesh axis runs over, the one named last changes fastest.
Arguments:
- features: bfloat16 [32, 4, 256, 1024], P(None, None, 'gx', 'gy'), may hold values from -8 to 8
- vessel_label: int32 [4, 256, 1024], P(None, 'gx', 'gy'), may hold values from 0 to 1, as said below
- conv_weight: bfloat16 [27, 32], replicated, may hold values from -0.21875 to 0.21875
- conv_bias: float32 [1], replicated, may hold values from -1.5 to 1.5
Outputs:
- cldice_loss: float32 [], replicated
- weight_grad: float32 [27, 32], replicated
- bias_grad: float32 [1], replicated
- feature_grad: bfloat16 [32, 4, 256, 1024], P(None, None, 'gx', 'gy')
Inputs may be any that keep to these rules, and one draw needn't show every extreme that they name: `vessel_label`: 1 marks a vessel voxel, 0 the background.
All inputs are finite; a program needn't handle non-finite values.
Results may differ from a plain program's by a relative error of at most 0.012.
Values may be sent and summed in bfloat16 or wider, within the bound.
No kernel may reach another device: no remote copies, remote signals or barrier semaphores. Data moves between devices by JAX's collectives and lax.ppermute only.
A program may use at most 64 MiB of HBM per device.

v0:
```python
import jax
import jax.numpy as jnp
from jax import lax
from jax.sharding import PartitionSpec as P

ITERS = 5
softmin_sharpness = 0.1
softness = 0.05


def padded_2(x, sides, width):
    for axis, dim in sides:
        size, length = (lax.axis_size(axis), x.shape[dim])
        up = [(i, (i + 1) % size) for i in range(size - 1)]
        down = [(j, i) for i, j in up]
        last = lax.slice_in_dim(x, length - width, length, axis=dim)
        initial = lax.slice_in_dim(x, 0, width, axis=dim)
        before = lax.ppermute(last, axis, up)
        after = lax.ppermute(initial, axis, down)
        x = jnp.concatenate([before, x, after], axis=dim)
    return x


def passed_along(value, axis, steps):
    count = lax.axis_size(axis)
    initial, last = (max(0, -steps), min(count, count - steps))
    return lax.ppermute(value, axis, [(source, source + steps) for source in range(initial, last)])


def soft_relu(source_grid):
    return softness * jax.nn.softplus(source_grid / softness)


def crop_cycle(array, amount):
    if amount == 0:
        return array
    return array[..., amount : array.shape[-2] - amount, amount : array.shape[-1] - amount]


def border_thickness(source_grid):
    widths = [(0, 0)] * (source_grid.ndim - 3) + [(1, 1), (0, 0), (0, 0)]
    return jnp.pad(source_grid, widths)


def soft_dilate(source_grid, cell_neighbourhood):
    scaled_powers = jnp.exp(border_thickness(source_grid) / softmin_sharpness)
    collapsed_aggregate = scaled_powers[:-2] + scaled_powers[1:-1] + scaled_powers[2:]
    collapsed_aggregate = (
        collapsed_aggregate[:, :-2] + collapsed_aggregate[:, 1:-1] + collapsed_aggregate[:, 2:]
    )
    collapsed_aggregate = (
        collapsed_aggregate[:, :, :-2]
        + collapsed_aggregate[:, :, 1:-1]
        + collapsed_aggregate[:, :, 2:]
    )
    return softmin_sharpness * jnp.log(collapsed_aggregate / 27.0) * cell_neighbourhood


def soft_erode(source_grid, cell_neighbourhood):
    scaled_powers = jnp.exp(-border_thickness(source_grid) / softmin_sharpness)
    middle_cell = scaled_powers[1:-1, 1:-1, 1:-1]
    neighbouring_cells = (
        scaled_powers[2:, 1:-1, 1:-1]
        + scaled_powers[:-2, 1:-1, 1:-1]
        + scaled_powers[1:-1, 2:, 1:-1]
        + scaled_powers[1:-1, :-2, 1:-1]
        + scaled_powers[1:-1, 1:-1, 2:]
        + scaled_powers[1:-1, 1:-1, :-2]
    )
    return (
        -softmin_sharpness
        * jnp.log(middle_cell / 3.0 + neighbouring_cells / 9.0)
        * cell_neighbourhood
    )


def soft_open(source_grid, cell_neighbourhood):
    return soft_dilate(
        soft_erode(source_grid, crop_cycle(cell_neighbourhood, 1)),
        crop_cycle(cell_neighbourhood, 2),
    )


def skeleton(source_grid, cell_neighbourhood, cycle_width):
    current = source_grid
    mask_now = cell_neighbourhood
    opened = soft_open(crop_cycle(current, cycle_width - 2), crop_cycle(mask_now, cycle_width - 2))
    skeleton_sum = soft_relu(crop_cycle(current, cycle_width) - opened)
    for erosion in range(1, cycle_width - 1):
        mask_now = crop_cycle(mask_now, 1)
        current = soft_erode(current, mask_now)
        cycle_now = cycle_width - erosion
        opened = soft_open(crop_cycle(current, cycle_now - 2), crop_cycle(mask_now, cycle_now - 2))
        change_term = soft_relu(crop_cycle(current, cycle_now) - opened)
        skeleton_sum = skeleton_sum + soft_relu(change_term - skeleton_sum * change_term)
    return skeleton_sum


def topology_loss(totals):
    precision = (totals[0] + 1.0) / (totals[1] + 1.0)
    sensitivity = (totals[2] + 1.0) / (totals[3] + 1.0)
    return 1.0 - 2.0 * precision * sensitivity / (precision + sensitivity)


def inside_mask(cycle_width, tile_rows, tile_cols):
    row_start = lax.axis_index("gx") * tile_rows - cycle_width
    col_start = lax.axis_index("gy") * tile_cols - cycle_width
    row_ids = row_start + jnp.arange(tile_rows + 2 * cycle_width, dtype=jnp.int32)
    col_ids = col_start + jnp.arange(tile_cols + 2 * cycle_width, dtype=jnp.int32)
    row_inside = (row_ids >= 0) & (row_ids < tile_rows * lax.axis_size("gx"))
    col_inside = (col_ids >= 0) & (col_ids < tile_cols * lax.axis_size("gy"))
    return (row_inside[:, None] & col_inside[None, :]).astype(jnp.float32)


def intersection_sums(prob_cycle, label_cycle, label_skeleton, cell_neighbourhood, cycle_width):
    pred_skeleton = skeleton(prob_cycle, cell_neighbourhood, cycle_width)
    prob_own = crop_cycle(prob_cycle, cycle_width)
    label_own = crop_cycle(label_cycle, cycle_width)
    return (
        jnp.sum(pred_skeleton * label_own),
        jnp.sum(pred_skeleton),
        jnp.sum(label_skeleton * prob_own),
        jnp.sum(label_skeleton),
    )


def extend(block, halo_width):
    return padded_2(block, (("gx", 2), ("gy", 3)), halo_width)


def convolve(feature_cycle, conv_weight, conv_bias):
    padded = border_thickness(feature_cycle)
    products = jnp.einsum("kc,czxy->kzxy", conv_weight, padded, preferred_element_type=jnp.float32)
    depth_cells = feature_cycle.shape[1]
    out_rows = feature_cycle.shape[2] - 2
    out_cols = feature_cycle.shape[3] - 2
    logits = jnp.zeros((depth_cells, out_rows, out_cols), jnp.float32) + conv_bias[0]
    for position in range(27):
        depth_shift, row_shift, col_shift = (position // 9, position // 3 % 3, position % 3)
        logits = (
            logits
            + products[
                position,
                depth_shift : depth_shift + depth_cells,
                row_shift : row_shift + out_rows,
                col_shift : col_shift + out_cols,
            ]
        )
    return (padded, logits)


def shifted_stack(grad_logits):
    pieces = []
    for position in range(27):
        depth_shift, row_shift, col_shift = (position // 9, position // 3 % 3, position % 3)
        pieces.append(
            jnp.pad(
                grad_logits,
                (
                    (depth_shift, 2 - depth_shift),
                    (row_shift, 2 - row_shift),
                    (col_shift, 2 - col_shift),
                ),
            )
        )
    stacked = jnp.stack(pieces)
    upper_part = stacked.astype(jnp.bfloat16)
    lower_part = (stacked - upper_part.astype(jnp.float32)).astype(jnp.bfloat16)
    return (upper_part, lower_part)


def weight_terms(upper_part, lower_part, padded):
    first = jnp.einsum("kzxy,czxy->kc", upper_part, padded, preferred_element_type=jnp.float32)
    return first + jnp.einsum(
        "kzxy,czxy->kc", lower_part, padded, preferred_element_type=jnp.float32
    )


def feature_terms(upper_part, lower_part, conv_weight):
    first = jnp.einsum("kc,kzxy->czxy", conv_weight, upper_part, preferred_element_type=jnp.float32)
    collapsed_aggregate = first + jnp.einsum(
        "kc,kzxy->czxy", conv_weight, lower_part, preferred_element_type=jnp.float32
    )
    return collapsed_aggregate[:, 1:-1]


def fold_back(gradient, halo_width):
    middle = gradient[..., halo_width : gradient.shape[-1] - halo_width]
    for shift_by in (1, -1):
        if shift_by == 1:
            rim_cells = gradient[..., gradient.shape[-1] - halo_width :]
        else:
            rim_cells = gradient[..., :halo_width]
        arrived = passed_along(rim_cells.astype(jnp.bfloat16), "gy", shift_by).astype(
            rim_cells.dtype
        )
        if shift_by == 1:
            middle = middle.at[..., :halo_width].add(arrived)
        else:
            middle = middle.at[..., middle.shape[-1] - halo_width :].add(arrived)
    result = middle[..., halo_width : middle.shape[-2] - halo_width, :]
    for shift_by in (1, -1):
        if shift_by == 1:
            rim_cells = middle[..., middle.shape[-2] - halo_width :, :]
        else:
            rim_cells = middle[..., :halo_width, :]
        arrived = passed_along(rim_cells.astype(jnp.bfloat16), "gx", shift_by).astype(
            rim_cells.dtype
        )
        if shift_by == 1:
            result = result.at[..., :halo_width, :].add(arrived)
        else:
            result = result.at[..., result.shape[-2] - halo_width :, :].add(arrived)
    return result


def local(features, vessel_label, conv_weight, conv_bias):
    channels, depth_cells, tile_rows, tile_cols = features.shape
    voxels = float(depth_cells * tile_rows * lax.axis_size("gx") * tile_cols * lax.axis_size("gy"))
    skel_reach = ITERS + 2
    cell_neighbourhood = inside_mask(skel_reach, tile_rows, tile_cols)
    fold_width = skel_reach + 1
    joined = jnp.concatenate([features, vessel_label.astype(jnp.bfloat16)[None]], axis=0)
    widened = extend(joined, fold_width)
    padded, logits = convolve(widened[:channels], conv_weight, conv_bias)
    label_cycle = crop_cycle(widened[channels].astype(jnp.float32), 1)
    label_skeleton = skeleton(label_cycle, cell_neighbourhood, skel_reach)

    def local_sums(logit_field):
        prob_cycle = jax.nn.sigmoid(logit_field) * cell_neighbourhood
        return intersection_sums(
            prob_cycle, label_cycle, label_skeleton, cell_neighbourhood, skel_reach
        )

    partial_sums, pullback = jax.vjp(local_sums, logits)

    def backward(cotangents):
        return jnp.stack([pullback(entry)[0] for entry in cotangents])

    totals = lax.psum(jnp.stack(partial_sums), ("gx", "gy"))
    loss_value, slopes = jax.value_and_grad(topology_loss)(totals)
    grad_logits = backward([tuple((slopes[entry] for entry in range(4)))])[0]
    upper_part, lower_part = shifted_stack(grad_logits)
    local_weight = weight_terms(upper_part, lower_part, padded)
    weight_grad, bias_grad = lax.psum((local_weight, jnp.sum(grad_logits)[None]), ("gx", "gy"))
    grad_own = fold_back(feature_terms(upper_part, lower_part, conv_weight), fold_width) * voxels
    return (loss_value, weight_grad, bias_grad, grad_own.astype(jnp.bfloat16))


def solution(mesh):
    in_specs = (P(None, None, "gx", "gy"), P(None, "gx", "gy"), P(), P())
    out_specs = (P(), P(), P(), P(None, None, "gx", "gy"))
    return jax.shard_map(local, mesh=mesh, in_specs=in_specs, out_specs=out_specs, check_vma=False)
```

profile of v0, /device:TPU:1, one launch (start us, length us, event | category | flops | bytes accessed | tf_op | source)
XLA Modules:
  0.0 265.2 jit_solution(332422820204132034)
XLA Ops:
  0.6 0.7 convert_bitcast_fusion
  1.4 1.1 copy_dynamic-update-slice_fusion
  2.5 1.3 collective-permute-start.1
  3.8 5.0 %collective-permute-start = (bf16[33,4,8,128]{3,0,2,1:T(8,128)(2,1)S(1)}, bf16[33,4,8,128]{3,0,2,1:T(8,128)(2,1)S(1)}, u32[]{:S(2)}, u32[]{:S(2)}) collective-permute-start(bf16[33,4,8,128]{3,0,2,1:T(8,128)(2,1)S(1)} %constant_dynamic-update-slice_fusion), channel_id=1, source_target_pairs={{0,8},{8,16},{16,24},{24,32},{32,40},{40,48},{48,56},{56,64},{64,7... | collective-permute-start | bytes 811016 | tf_op jit(solution)/shard_map/ppermute | solution.py:18
  8.9 0.7 fusion.370
  9.6 0.7 fusion.371
  10.3 0.7 fusion.372
  10.9 0.7 fusion.373
  11.7 0.7 fusion.374
  12.4 0.9 collective-permute-done
  13.4 0.4 fusion.369
  13.7 1.3 copy.71
  15.1 0.6 copy.72
  15.7 5.3 %collective-permute-start.3 = (bf16[33,4,24,8]{0,3,2,1:T(8,128)(2,1)S(1)}, bf16[33,4,24,8]{0,3,2,1:T(8,128)(2,1)}, u32[]{:S(2)}, u32[]{:S(2)}) collective-permute-start(bf16[33,4,24,8]{0,3,2,1:T(8,128)(2,1)S(1)} %copy.72), channel_id=1, source_target_pairs={{1,0},{2,1},{3,2},{4,3},{5,4},{6,5},{7,6},{9,8},{10,9},{11,10},{12... | collective-permute-start | bytes 152072 | tf_op jit(solution)/shard_map/ppermute | solution.py:19
  21.1 3.0 %collective-permute-start.2 = (bf16[33,4,24,8]{0,3,2,1:T(8,128)(2,1)}, bf16[33,4,24,8]{0,3,2,1:T(8,128)(2,1)S(1)}, u32[]{:S(2)}, u32[]{:S(2)}) collective-permute-start(bf16[33,4,24,8]{0,3,2,1:T(8,128)(2,1)} %copy.71), channel_id=1, source_target_pairs={{0,1},{1,2},{2,3},{3,4},{4,5},{5,6},{6,7},{8,9},{9,10},{10,11},{11... | collective-permute-start | bytes 152072 | tf_op jit(solution)/shard_map/ppermute | solution.py:18
  24.8 2.2 collective-permute-done.2
  27.0 0.7 copy.73
  27.7 1.6 copy.74
  29.8 1.2 pad_maximum_fusion
  31.0 1.3 copy-done.2
  32.3 0.6 fusion.321
  33.0 2.3 copy.128
  35.3 0.6 broadcast_multiply_fusion.4
  36.0 0.4 log_multiply_fusion.1
  36.6 0.4 log_multiply_fusion
  39.4 0.9 log_multiply_fusion.3
  40.8 0.9 log_multiply_fusion.10
  41.8 0.9 log_multiply_fusion.4
  42.9 0.9 log_multiply_fusion.8
  44.0 1.5 multiply_reduce_fusion
  45.4 0.9 multiply_reduce_fusion.1
  46.3 2.6 pad_maximum_fusion.2
  48.9 83.7 %psum.21 = f32[4]{0:T(128)S(1)} all-reduce(f32[4]{0:T(128)S(1)} %pad_maximum_fusion.2), channel_id=1, replica_groups=mesh['gx'=32,'gy'=8] {'gx','gy'}, use_global_device_ids=true, to_apply=%region_4.6 | all-reduce | flops 4 | bytes 32 | tf_op jit(solution)/shard_map/psum | solution.py:240
  132.7 0.6 fusion.378
  136.2 0.7 fusion.377
  136.9 1.5 divide_multiply_fusion.5
  139.2 1.0 broadcast_multiply_fusion.15
  140.3 1.0 broadcast_multiply_fusion.16
  141.5 1.0 broadcast_multiply_fusion.5
  143.1 0.9 broadcast_multiply_fusion.7
  145.8 0.7 broadcast_multiply_fusion.25
  146.6 0.8 fusion.327
  149.3 0.6 subtract_convert_fusion
  149.8 1.8 fusion.5
  151.6 5.3 %fusion.379 = (bf16[32,6,24,144]{0,3,2,1:T(8,128)(2,1)S(1)}, f32[32,6,24,144]{0,3,2,1:T(8,128)}) fusion(f32[6,24,144,32]{3,2,1,0:T(8,128)S(1)} %fusion.5, bf16[27,32]{1,0:T(8,128)(2,1)S(1)} %copy-done, bf16[27,6,24,144]{3,2,1,0:T(8,128)(2,1)S(1)} %get-tuple-element.140), kind=kOutput, calls=%fused_computation.833 | convolution fusion | flops 37158912 | bytes 7756992 | tf_op jit(solution)/shard_map/kc,kzxy->czxy/dot_general | solution.py:181
  156.9 2.9 %collective-permute-start.4 = (bf16[32,4,24,8]{0,3,2,1:T(8,128)(2,1)S(1)}, bf16[32,4,24,8]{0,3,2,1:T(8,128)(2,1)S(1)}, u32[]{:S(2)}, u32[]{:S(2)}) collective-permute-start(bf16[32,4,24,8]{0,3,2,1:T(8,128)(2,1)S(1)} %get-tuple-element.213), channel_id=1, source_target_pairs={{0,1},{1,2},{2,3},{3,4},{4,5},{5,6},{6,7},{8,9},{9,10},{10,11},{11... | collective-permute-start | bytes 147464 | tf_op jit(solution)/shard_map/ppermute | solution.py:27
  159.8 1.3 fusion.17
  161.2 2.1 collective-permute-start.5
  163.3 3.2 %slice.1858 = f32[32,4,24,128]{0,3,2,1:T(8,128)S(1)} slice(f32[32,6,24,144]{0,3,2,1:T(8,128)} %get-tuple-element.273), slice={[0:32], [1:5], [0:24], [8:136]} | slice | bytes 3145728 | tf_op jit(solution)/shard_map/slice | solution.py:188
  166.6 1.0 fusion.28
  167.6 0.5 collective-permute-done.5
  168.3 0.7 convert.10
  169.0 1.9 copy-done.1
  170.9 1.1 fusion.368
  172.0 2.4 copy.86
  174.4 0.5 copy.88
  175.0 1.3 collective-permute-start.7
  176.3 4.3 %collective-permute-start.6 = (bf16[32,4,8,128]{3,2,1,0:T(8,128)(2,1)}, bf16[32,4,8,128]{3,2,1,0:T(8,128)(2,1)S(1)}, u32[]{:S(2)}, u32[]{:S(2)}) collective-permute-start(bf16[32,4,8,128]{3,2,1,0:T(8,128)(2,1)} %copy.86), channel_id=1, source_target_pairs={{0,8},{8,16},{16,24},{24,32},{32,40},{40,48},{48,56},{56,64},{64,7... | collective-permute-start | bytes 786440 | tf_op jit(solution)/shard_map/ppermute | solution.py:27
  180.6 2.7 %fusion.22 = f32[27,32]{1,0:T(8,128)S(1)} fusion(f32[27,32]{1,0:T(8,128)S(1)} %fusion.17, bf16[27,6,24,144]{3,2,1,0:T(8,128)(2,1)S(1)} %get-tuple-element.141, bf16[33,4,24,144]{3,0,2,1:T(8,128)(2,1)} %copy-done.2), kind=kOutput, calls=%fused_computation.19 | convolution fusion | flops 35832672 | bytes 2699520 | tf_op jit(solution)/shard_map/kzxy,czxy->kc/dot_general | solution.py:173
  183.3 76.3 %all-reduce.209 = (f32[27,32]{1,0:T(8,128)}, f32[1]{0:T(128)}) all-reduce(f32[27,32]{1,0:T(8,128)S(1)} %fusion.22, f32[1]{0:T(128)} %bitcast.63), channel_id=1, replica_groups=mesh['gx'=32,'gy'=8] {'gx','gy'}, use_global_device_ids=true, to_apply=%region_5.7 | all-reduce | flops 865 | bytes 6920 | tf_op jit(solution)/shard_map/psum | solution.py:245
  259.6 0.5 copy.87
  260.1 0.5 copy.89
  260.6 2.2 fusion.11
  262.8 1.3 copy.90
  (180 shorter events, 9.3 us)
Async XLA Ops:
  0.6 31.7 %copy-start = (bf16[27,32]{1,0:T(8,128)(2,1)S(1)}, bf16[27,32]{1,0:T(8,128)(2,1)}, u32[]{:S(2)}) copy-start(bf16[27,32]{1,0:T(8,128)(2,1)} %param.19) | copy-start | bytes 5188
  2.5 9.9 %collective-permute-start.1 = (bf16[33,4,8,128]{3,0,2,1:T(8,128)(2,1)S(1)}, bf16[33,4,8,128]{3,0,2,1:T(8,128)(2,1)S(1)}, u32[]{:S(2)}, u32[]{:S(2)}) collective-permute-start(bf16[33,4,8,128]{3,0,2,1:T(8,128)(2,1)S(1)} %constant_dynamic-update-slice_fusion), channel_id=1, source_target_pairs={{8,0},{16,8},{24,16},{32,24},{40,32},{48,40},{56,48},{64,56},{72,6... | collective-permute-start | bytes 811016 | tf_op jit(solution)/shard_map/ppermute | solution.py:19
  3.8 9.5 %collective-permute-start = (bf16[33,4,8,128]{3,0,2,1:T(8,128)(2,1)S(1)}, bf16[33,4,8,128]{3,0,2,1:T(8,128)(2,1)S(1)}, u32[]{:S(2)}, u32[]{:S(2)}) collective-permute-start(bf16[33,4,8,128]{3,0,2,1:T(8,128)(2,1)S(1)} %constant_dynamic-update-slice_fusion), channel_id=1, source_target_pairs={{0,8},{8,16},{16,24},{24,32},{32,40},{40,48},{48,56},{56,64},{64,7... | collective-permute-start | bytes 811016 | tf_op jit(solution)/shard_map/ppermute | solution.py:18
  15.7 12.0 %collective-permute-start.3 = (bf16[33,4,24,8]{0,3,2,1:T(8,128)(2,1)S(1)}, bf16[33,4,24,8]{0,3,2,1:T(8,128)(2,1)}, u32[]{:S(2)}, u32[]{:S(2)}) collective-permute-start(bf16[33,4,24,8]{0,3,2,1:T(8,128)(2,1)S(1)} %copy.72), channel_id=1, source_target_pairs={{1,0},{2,1},{3,2},{4,3},{5,4},{6,5},{7,6},{9,8},{10,9},{11,10},{12... | collective-permute-start | bytes 152072 | tf_op jit(solution)/shard_map/ppermute | solution.py:19
  21.1 5.9 %collective-permute-start.2 = (bf16[33,4,24,8]{0,3,2,1:T(8,128)(2,1)}, bf16[33,4,24,8]{0,3,2,1:T(8,128)(2,1)S(1)}, u32[]{:S(2)}, u32[]{:S(2)}) collective-permute-start(bf16[33,4,24,8]{0,3,2,1:T(8,128)(2,1)} %copy.71), channel_id=1, source_target_pairs={{0,1},{1,2},{2,3},{3,4},{4,5},{5,6},{6,7},{8,9},{9,10},{10,11},{11... | collective-permute-start | bytes 152072 | tf_op jit(solution)/shard_map/ppermute | solution.py:18
  31.0 1.3 copy-start.2
  35.8 1.9 copy-start.8
  37.7 1.7 copy-start.7
  44.0 96.3 %copy-start.4 = (f32[4,10,130]{2,1,0:T(8,128)S(1)}, f32[4,10,130]{2,1,0:T(8,128)}, u32[]{:S(2)}) copy-start(f32[4,10,130]{2,1,0:T(8,128)} %get-tuple-element.198) | copy-start | bytes 62404
  45.4 98.8 %copy-start.9 = (f32[16,136]{1,0:T(8,128)S(1)}, f32[16,136]{1,0:T(8,128)}, u32[]{:S(2)}) copy-start(f32[16,136]{1,0:T(8,128)} %get-tuple-element.230) | copy-start | bytes 26116
  138.9 6.1 %copy-start.6 = (f32[18,138]{1,0:T(8,128)S(1)}, f32[18,138]{1,0:T(8,128)}, u32[]{:S(2)}) copy-start(f32[18,138]{1,0:T(8,128)} %get-tuple-element.232) | copy-start | bytes 29812
  140.2 5.2 %copy-start.5 = (f32[20,140]{1,0:T(8,128)S(1)}, f32[20,140]{1,0:T(8,128)}, u32[]{:S(2)}) copy-start(f32[20,140]{1,0:T(8,128)} %get-tuple-element.234) | copy-start | bytes 33604
  141.3 4.5 %copy-start.10 = (f32[4,8,128]{2,1,0:T(8,128)S(1)}, f32[4,8,128]{2,1,0:T(8,128)}, u32[]{:S(2)}) copy-start(f32[4,8,128]{2,1,0:T(8,128)} %get-tuple-element.209) | copy-start | bytes 49156
  151.6 8.2 %copy-start.3 = (bf16[33,4,24,144]{3,0,2,1:T(8,128)(2,1)S(1)}, bf16[33,4,24,144]{3,0,2,1:T(8,128)(2,1)}, u32[]{:S(2)}) copy-start(bf16[33,4,24,144]{3,0,2,1:T(8,128)(2,1)} %copy-done.2) | copy-start | bytes 2737156
  156.9 9.6 %collective-permute-start.4 = (bf16[32,4,24,8]{0,3,2,1:T(8,128)(2,1)S(1)}, bf16[32,4,24,8]{0,3,2,1:T(8,128)(2,1)S(1)}, u32[]{:S(2)}, u32[]{:S(2)}) collective-permute-start(bf16[32,4,24,8]{0,3,2,1:T(8,128)(2,1)S(1)} %get-tuple-element.213), channel_id=1, source_target_pairs={{0,1},{1,2},{2,3},{3,4},{4,5},{5,6},{6,7},{8,9},{9,10},{10,11},{11... | collective-permute-start | bytes 147464 | tf_op jit(solution)/shard_map/ppermute | solution.py:27
  161.2 7.0 %collective-permute-start.5 = (bf16[32,4,24,8]{0,3,2,1:T(8,128)(2,1)S(1)}, bf16[32,4,24,8]{0,3,2,1:T(8,128)(2,1)S(1)}, u32[]{:S(2)}, u32[]{:S(2)}) collective-permute-start(bf16[32,4,24,8]{0,3,2,1:T(8,128)(2,1)S(1)} %get-tuple-element.212), channel_id=1, source_target_pairs={{1,0},{2,1},{3,2},{4,3},{5,4},{6,5},{7,6},{9,8},{10,9},{11,10},{12... | collective-permute-start | bytes 147464 | tf_op jit(solution)/shard_map/ppermute | solution.py:27
  168.3 2.6 copy-start.1
  175.0 85.1 %collective-permute-start.7 = (bf16[32,4,8,128]{3,2,1,0:T(8,128)(2,1)S(1)}, bf16[32,4,8,128]{3,2,1,0:T(8,128)(2,1)S(1)}, u32[]{:S(2)}, u32[]{:S(2)}) collective-permute-start(bf16[32,4,8,128]{3,2,1,0:T(8,128)(2,1)S(1)} %copy.88), channel_id=1, source_target_pairs={{8,0},{16,8},{24,16},{32,24},{40,32},{48,40},{56,48},{64,56},{72,6... | collective-permute-start | bytes 786440 | tf_op jit(solution)/shard_map/ppermute | solution.py:27
  176.3 83.3 %collective-permute-start.6 = (bf16[32,4,8,128]{3,2,1,0:T(8,128)(2,1)}, bf16[32,4,8,128]{3,2,1,0:T(8,128)(2,1)S(1)}, u32[]{:S(2)}, u32[]{:S(2)}) collective-permute-start(bf16[32,4,8,128]{3,2,1,0:T(8,128)(2,1)} %copy.86), channel_id=1, source_target_pairs={{0,8},{8,16},{16,24},{24,32},{32,40},{40,48},{48,56},{56,64},{64,7... | collective-permute-start | bytes 786440 | tf_op jit(solution)/shard_map/ppermute | solution.py:27
where the time goes:
time: 266 us; the launch traced here: 265 us
  blocking collectives  160 us (60%)
  other arithmetic  33 us (12%)
  starting transfers between devices  25.3 us (10%)
  local copies, waits for them, and re-layouts  24.9 us (9%)
  matrix products  11.7 us (4%)
  between operations  6.76 us (3%)
  waiting for transfers between devices  3.59 us (1%)
    psum x1, blocking collectives, local(): totals = lax.psum(jnp.stack(partial_sums), ('gx', 'gy'))  83.7 us
    psum x1, blocking collectives, local(): lax.psum((local_weight, jnp.sum(grad_logits)[None]), ('gx', 'gy'))  76.3 us
    ppermute x4, starting transfers between devices, passed_along(): lax.ppermute(value, axis, [(source, source + steps) for source in range(i...  10.6 us
    ppermute x2, starting transfers between devices, padded_2(): before = lax.ppermute(last, axis, up)  8.04 us
    unnamed x51, local copies, waits for them, and re-layouts  7.28 us
    ppermute x2, starting transfers between devices, padded_2(): after = lax.ppermute(initial, axis, down)  6.62 us
    mul x11, other arithmetic, soft_erode(): -softmin_sharpness * jnp.log(middle_cell / 3.0 + neighbouring_cells / 9.0)  5.88 us
  transfers between devices with their start and end apart: 8, of which 3 were waited for; matrix products, arithmetic and copies ran while one was open for 5% of the time, Pallas kernels for 0%

commit v1 on v0

--- a/solution.py
+++ b/solution.py
@@ -237,7 +237,7 @@
     def backward(cotangents):
         return jnp.stack([pullback(entry)[0] for entry in cotangents])
 
-    totals = lax.psum(jnp.stack(partial_sums), ("gx", "gy"))
+    totals = lax.psum(lax.psum(jnp.stack(partial_sums), "gy"), "gx")
     loss_value, slopes = jax.value_and_grad(topology_loss)(totals)
     grad_logits = backward([tuple((slopes[entry] for entry in range(4)))])[0]
     upper_part, lower_part = shifted_stack(grad_logits)

time: 266 us -> 271 us (1.019)
  starting transfers between devices: 25.3 us -> 38.2 us
  blocking collectives: 160 us -> 152 us
    ppermute x4, starting transfers between devices: 10.6 us -> 23.5 us  [passed_along(): lax.ppermute(value, axis, [(source, source + steps) for source in range(i...]
    psum x1 -> x2, blocking collectives: 83.7 us -> 78.1 us  [local(): totals = lax.psum(lax.psum(jnp.stack(partial_sums), 'gy'), 'gx')]
where the time goes in v1:
time: 271 us; the launch traced here: 270 us
  blocking collectives  152 us (56%)
  starting transfers between devices  38.2 us (14%)
  other arithmetic  33 us (12%)
  local copies, waits for them, and re-layouts  24.9 us (9%)
  matrix products  11.7 us (4%)
  between operations  6.8 us (3%)
  waiting for transfers between devices  3.29 us (1%)
    psum x2, blocking collectives, local(): totals = lax.psum(lax.psum(jnp.stack(partial_sums), 'gy'), 'gx')  78.1 us
    psum x1, blocking collectives, local(): lax.psum((local_weight, jnp.sum(grad_logits)[None]), ('gx', 'gy'))  74 us
    ppermute x4, starting transfers between devices, passed_along(): lax.ppermute(value, axis, [(source, source + steps) for source in range(i...  23.5 us
    ppermute x2, starting transfers between devices, padded_2(): before = lax.ppermute(last, axis, up)  8.04 us
    unnamed x51, local copies, waits for them, and re-layouts  7.24 us
    ppermute x2, starting transfers between devices, padded_2(): after = lax.ppermute(initial, axis, down)  6.62 us
    mul x11, other arithmetic, soft_erode(): -softmin_sharpness * jnp.log(middle_cell / 3.0 + neighbouring_cells / 9.0)  5.84 us
  transfers between devices with their start and end apart: 8, of which 3 were waited for; matrix products, arithmetic and copies ran while one was open for 5% of the time, Pallas kernels for 0%

profile of v1, /device:TPU:1, one launch (start us, length us, event | category | flops | bytes accessed | tf_op | source)
XLA Modules:
  0.0 269.9 jit_solution(8864720336116154564)
XLA Ops:
  0.6 0.7 convert_bitcast_fusion
  1.4 1.1 copy_dynamic-update-slice_fusion
  2.5 1.3 collective-permute-start.1
  3.8 5.0 %collective-permute-start = (bf16[33,4,8,128]{3,0,2,1:T(8,128)(2,1)S(1)}, bf16[33,4,8,128]{3,0,2,1:T(8,128)(2,1)S(1)}, u32[]{:S(2)}, u32[]{:S(2)}) collective-permute-start(bf16[33,4,8,128]{3,0,2,1:T(8,128)(2,1)S(1)} %constant_dynamic-update-slice_fusion), channel_id=1, source_target_pairs={{0,8},{8,16},{16,24},{24,32},{32,40},{40,48},{48,56},{56,64},{64,7... | collective-permute-start | bytes 811016 | tf_op jit(solution)/shard_map/ppermute | solution.py:18
  8.9 0.7 fusion.370
  9.6 0.7 fusion.371
  10.3 0.7 fusion.372
  10.9 0.7 fusion.373
  11.7 0.7 fusion.374
  12.4 0.9 collective-permute-done
  13.4 0.4 fusion.369
  13.7 1.3 copy.71
  15.1 0.6 copy.72
  15.7 5.3 %collective-permute-start.3 = (bf16[33,4,24,8]{0,3,2,1:T(8,128)(2,1)S(1)}, bf16[33,4,24,8]{0,3,2,1:T(8,128)(2,1)}, u32[]{:S(2)}, u32[]{:S(2)}) collective-permute-start(bf16[33,4,24,8]{0,3,2,1:T(8,128)(2,1)S(1)} %copy.72), channel_id=1, source_target_pairs={{1,0},{2,1},{3,2},{4,3},{5,4},{6,5},{7,6},{9,8},{10,9},{11,10},{12... | collective-permute-start | bytes 152072 | tf_op jit(solution)/shard_map/ppermute | solution.py:19
  21.1 3.0 %collective-permute-start.2 = (bf16[33,4,24,8]{0,3,2,1:T(8,128)(2,1)}, bf16[33,4,24,8]{0,3,2,1:T(8,128)(2,1)S(1)}, u32[]{:S(2)}, u32[]{:S(2)}) collective-permute-start(bf16[33,4,24,8]{0,3,2,1:T(8,128)(2,1)} %copy.71), channel_id=1, source_target_pairs={{0,1},{1,2},{2,3},{3,4},{4,5},{5,6},{6,7},{8,9},{9,10},{10,11},{11... | collective-permute-start | bytes 152072 | tf_op jit(solution)/shard_map/ppermute | solution.py:18
  24.8 2.2 collective-permute-done.2
  27.0 0.7 copy.73
  27.7 1.6 copy.74
  29.8 1.2 pad_maximum_fusion
  31.0 1.3 copy-done.2
  32.3 0.6 fusion.321
  32.9 2.3 copy.128
  35.3 0.6 broadcast_multiply_fusion.4
  36.0 0.4 log_multiply_fusion.1
  36.6 0.4 log_multiply_fusion
  39.4 0.9 log_multiply_fusion.3
  40.8 0.9 log_multiply_fusion.10
  41.8 0.9 log_multiply_fusion.4
  42.8 0.9 log_multiply_fusion.8
  43.9 1.5 multiply_reduce_fusion
  45.4 0.9 multiply_reduce_fusion.1
  46.3 2.7 pad_maximum_fusion.2
  48.9 13.0 %psum.28 = f32[4]{0:T(128)S(1)} all-reduce(f32[4]{0:T(128)S(1)} %pad_maximum_fusion.2), channel_id=1, replica_groups=mesh['gx'=32,'gy'=8] {'gy'}, use_global_device_ids=true, to_apply=%region_4.6 | all-reduce | flops 4 | bytes 32 | tf_op jit(solution)/shard_map/psum | solution.py:240
  61.9 65.2 %psum.29 = f32[4]{0:T(128)S(1)} all-reduce(f32[4]{0:T(128)S(1)} %psum.28), channel_id=1, replica_groups=mesh['gx'=32,'gy'=8] {'gx'}, use_global_device_ids=true, to_apply=%region_5.7 | all-reduce | flops 4 | bytes 32 | tf_op jit(solution)/shard_map/psum | solution.py:240
  127.1 0.7 fusion.378
  130.7 0.7 fusion.377
  131.4 1.5 divide_multiply_fusion.5
  133.7 1.0 broadcast_multiply_fusion.15
  134.9 1.0 broadcast_multiply_fusion.16
  136.1 1.0 broadcast_multiply_fusion.5
  137.7 0.9 broadcast_multiply_fusion.7
  140.4 0.7 broadcast_multiply_fusion.25
  141.1 0.8 fusion.327
  143.8 0.6 subtract_convert_fusion
  144.4 1.8 fusion.5
  146.2 5.3 %fusion.379 = (bf16[32,6,24,144]{0,3,2,1:T(8,128)(2,1)S(1)}, f32[32,6,24,144]{0,3,2,1:T(8,128)}) fusion(f32[6,24,144,32]{3,2,1,0:T(8,128)S(1)} %fusion.5, bf16[27,32]{1,0:T(8,128)(2,1)S(1)} %copy-done, bf16[27,6,24,144]{3,2,1,0:T(8,128)(2,1)S(1)} %get-tuple-element.140), kind=kOutput, calls=%fused_computation.833 | convolution fusion | flops 37158912 | bytes 7756992 | tf_op jit(solution)/shard_map/kc,kzxy->czxy/dot_general | solution.py:181
  151.5 15.5 %collective-permute-start.4 = (bf16[32,4,24,8]{0,3,2,1:T(8,128)(2,1)S(1)}, bf16[32,4,24,8]{0,3,2,1:T(8,128)(2,1)S(1)}, u32[]{:S(2)}, u32[]{:S(2)}) collective-permute-start(bf16[32,4,24,8]{0,3,2,1:T(8,128)(2,1)S(1)} %get-tuple-element.213), channel_id=1, source_target_pairs={{0,1},{1,2},{2,3},{3,4},{4,5},{5,6},{6,7},{8,9},{9,10},{10,11},{11... | collective-permute-start | bytes 147464 | tf_op jit(solution)/shard_map/ppermute | solution.py:27
  167.0 1.3 fusion.17
  168.4 2.5 collective-permute-start.5
  170.9 3.2 %slice.1858 = f32[32,4,24,128]{0,3,2,1:T(8,128)S(1)} slice(f32[32,6,24,144]{0,3,2,1:T(8,128)} %get-tuple-element.273), slice={[0:32], [1:5], [0:24], [8:136]} | slice | bytes 3145728 | tf_op jit(solution)/shard_map/slice | solution.py:188
  174.1 1.0 fusion.28
  175.5 0.7 convert.10
  176.2 1.9 copy-done.1
  178.1 1.1 fusion.368
  179.2 2.4 copy.86
  181.6 0.5 copy.88
  182.1 1.3 collective-permute-start.7
  183.4 4.2 %collective-permute-start.6 = (bf16[32,4,8,128]{3,2,1,0:T(8,128)(2,1)}, bf16[32,4,8,128]{3,2,1,0:T(8,128)(2,1)S(1)}, u32[]{:S(2)}, u32[]{:S(2)}) collective-permute-start(bf16[32,4,8,128]{3,2,1,0:T(8,128)(2,1)} %copy.86), channel_id=1, source_target_pairs={{0,8},{8,16},{16,24},{24,32},{32,40},{40,48},{48,56},{56,64},{64,7... | collective-permute-start | bytes 786440 | tf_op jit(solution)/shard_map/ppermute | solution.py:27
  187.7 2.7 fusion.22
  190.4 74.0 %all-reduce.209 = (f32[27,32]{1,0:T(8,128)}, f32[1]{0:T(128)}) all-reduce(f32[27,32]{1,0:T(8,128)S(1)} %fusion.22, f32[1]{0:T(128)} %bitcast.63), channel_id=1, replica_groups=mesh['gx'=32,'gy'=8] {'gx','gy'}, use_global_device_ids=true, to_apply=%region_6.8 | all-reduce | flops 865 | bytes 6920 | tf_op jit(solution)/shard_map/psum | solution.py:245
  264.3 0.5 copy.87
  264.9 0.5 copy.89
  265.4 2.2 fusion.11
  267.6 1.3 copy.90
  (181 shorter events, 9.5 us)
Async XLA Ops:
  0.6 31.7 %copy-start = (bf16[27,32]{1,0:T(8,128)(2,1)S(1)}, bf16[27,32]{1,0:T(8,128)(2,1)}, u32[]{:S(2)}) copy-start(bf16[27,32]{1,0:T(8,128)(2,1)} %param.19) | copy-start | bytes 5188
  2.5 9.9 %collective-permute-start.1 = (bf16[33,4,8,128]{3,0,2,1:T(8,128)(2,1)S(1)}, bf16[33,4,8,128]{3,0,2,1:T(8,128)(2,1)S(1)}, u32[]{:S(2)}, u32[]{:S(2)}) collective-permute-start(bf16[33,4,8,128]{3,0,2,1:T(8,128)(2,1)S(1)} %constant_dynamic-update-slice_fusion), channel_id=1, source_target_pairs={{8,0},{16,8},{24,16},{32,24},{40,32},{48,40},{56,48},{64,56},{72,6... | collective-permute-start | bytes 811016 | tf_op jit(solution)/shard_map/ppermute | solution.py:19
  3.8 9.5 %collective-permute-start = (bf16[33,4,8,128]{3,0,2,1:T(8,128)(2,1)S(1)}, bf16[33,4,8,128]{3,0,2,1:T(8,128)(2,1)S(1)}, u32[]{:S(2)}, u32[]{:S(2)}) collective-permute-start(bf16[33,4,8,128]{3,0,2,1:T(8,128)(2,1)S(1)} %constant_dynamic-update-slice_fusion), channel_id=1, source_target_pairs={{0,8},{8,16},{16,24},{24,32},{32,40},{40,48},{48,56},{56,64},{64,7... | collective-permute-start | bytes 811016 | tf_op jit(solution)/shard_map/ppermute | solution.py:18
  15.7 12.0 %collective-permute-start.3 = (bf16[33,4,24,8]{0,3,2,1:T(8,128)(2,1)S(1)}, bf16[33,4,24,8]{0,3,2,1:T(8,128)(2,1)}, u32[]{:S(2)}, u32[]{:S(2)}) collective-permute-start(bf16[33,4,24,8]{0,3,2,1:T(8,128)(2,1)S(1)} %copy.72), channel_id=1, source_target_pairs={{1,0},{2,1},{3,2},{4,3},{5,4},{6,5},{7,6},{9,8},{10,9},{11,10},{12... | collective-permute-start | bytes 152072 | tf_op jit(solution)/shard_map/ppermute | solution.py:19
  21.1 5.9 %collective-permute-start.2 = (bf16[33,4,24,8]{0,3,2,1:T(8,128)(2,1)}, bf16[33,4,24,8]{0,3,2,1:T(8,128)(2,1)S(1)}, u32[]{:S(2)}, u32[]{:S(2)}) collective-permute-start(bf16[33,4,24,8]{0,3,2,1:T(8,128)(2,1)} %copy.71), channel_id=1, source_target_pairs={{0,1},{1,2},{2,3},{3,4},{4,5},{5,6},{6,7},{8,9},{9,10},{10,11},{11... | collective-permute-start | bytes 152072 | tf_op jit(solution)/shard_map/ppermute | solution.py:18
  31.0 1.3 copy-start.2
  35.8 1.9 copy-start.8
  37.7 1.7 copy-start.7
  43.9 91.0 %copy-start.4 = (f32[4,10,130]{2,1,0:T(8,128)S(1)}, f32[4,10,130]{2,1,0:T(8,128)}, u32[]{:S(2)}) copy-start(f32[4,10,130]{2,1,0:T(8,128)} %get-tuple-element.198) | copy-start | bytes 62404
  45.4 93.4 %copy-start.9 = (f32[16,136]{1,0:T(8,128)S(1)}, f32[16,136]{1,0:T(8,128)}, u32[]{:S(2)}) copy-start(f32[16,136]{1,0:T(8,128)} %get-tuple-element.230) | copy-start | bytes 26116
  133.4 6.1 %copy-start.6 = (f32[18,138]{1,0:T(8,128)S(1)}, f32[18,138]{1,0:T(8,128)}, u32[]{:S(2)}) copy-start(f32[18,138]{1,0:T(8,128)} %get-tuple-element.232) | copy-start | bytes 29812
  134.7 5.2 %copy-start.5 = (f32[20,140]{1,0:T(8,128)S(1)}, f32[20,140]{1,0:T(8,128)}, u32[]{:S(2)}) copy-start(f32[20,140]{1,0:T(8,128)} %get-tuple-element.234) | copy-start | bytes 33604
  135.8 4.5 %copy-start.10 = (f32[4,8,128]{2,1,0:T(8,128)S(1)}, f32[4,8,128]{2,1,0:T(8,128)}, u32[]{:S(2)}) copy-start(f32[4,8,128]{2,1,0:T(8,128)} %get-tuple-element.209) | copy-start | bytes 49156
  146.2 20.9 %copy-start.3 = (bf16[33,4,24,144]{3,0,2,1:T(8,128)(2,1)S(1)}, bf16[33,4,24,144]{3,0,2,1:T(8,128)(2,1)}, u32[]{:S(2)}) copy-start(bf16[33,4,24,144]{3,0,2,1:T(8,128)(2,1)} %copy-done.2) | copy-start | bytes 2737156
  151.5 22.6 %collective-permute-start.4 = (bf16[32,4,24,8]{0,3,2,1:T(8,128)(2,1)S(1)}, bf16[32,4,24,8]{0,3,2,1:T(8,128)(2,1)S(1)}, u32[]{:S(2)}, u32[]{:S(2)}) collective-permute-start(bf16[32,4,24,8]{0,3,2,1:T(8,128)(2,1)S(1)} %get-tuple-element.213), channel_id=1, source_target_pairs={{0,1},{1,2},{2,3},{3,4},{4,5},{5,6},{6,7},{8,9},{9,10},{10,11},{11... | collective-permute-start | bytes 147464 | tf_op jit(solution)/shard_map/ppermute | solution.py:27
  168.4 7.0 %collective-permute-start.5 = (bf16[32,4,24,8]{0,3,2,1:T(8,128)(2,1)S(1)}, bf16[32,4,24,8]{0,3,2,1:T(8,128)(2,1)S(1)}, u32[]{:S(2)}, u32[]{:S(2)}) collective-permute-start(bf16[32,4,24,8]{0,3,2,1:T(8,128)(2,1)S(1)} %get-tuple-element.212), channel_id=1, source_target_pairs={{1,0},{2,1},{3,2},{4,3},{5,4},{6,5},{7,6},{9,8},{10,9},{11,10},{12... | collective-permute-start | bytes 147464 | tf_op jit(solution)/shard_map/ppermute | solution.py:27
  175.5 2.6 copy-start.1
  182.1 82.7 %collective-permute-start.7 = (bf16[32,4,8,128]{3,2,1,0:T(8,128)(2,1)S(1)}, bf16[32,4,8,128]{3,2,1,0:T(8,128)(2,1)S(1)}, u32[]{:S(2)}, u32[]{:S(2)}) collective-permute-start(bf16[32,4,8,128]{3,2,1,0:T(8,128)(2,1)S(1)} %copy.88), channel_id=1, source_target_pairs={{8,0},{16,8},{24,16},{32,24},{40,32},{48,40},{56,48},{64,56},{72,6... | collective-permute-start | bytes 786440 | tf_op jit(solution)/shard_map/ppermute | solution.py:27
  183.4 80.9 %collective-permute-start.6 = (bf16[32,4,8,128]{3,2,1,0:T(8,128)(2,1)}, bf16[32,4,8,128]{3,2,1,0:T(8,128)(2,1)S(1)}, u32[]{:S(2)}, u32[]{:S(2)}) collective-permute-start(bf16[32,4,8,128]{3,2,1,0:T(8,128)(2,1)} %copy.86), channel_id=1, source_target_pairs={{0,8},{8,16},{16,24},{24,32},{32,40},{40,48},{48,56},{56,64},{64,7... | collective-permute-start | bytes 786440 | tf_op jit(solution)/shard_map/ppermute | solution.py:27
